TPU v7x, 512 devices: a whole 4x8x8 slice. The times are simulated.
512 devices in a mesh: train: 32 (over z, x_lo, core), query: 16 (over x_hi, y).
Axes of the slice: x: 4 (x_hi: 2, x_lo: 2; x = x_hi * 2 + x_lo), y: 8, z: 8, core: 2. Of those that a mesh axis runs over, the one named last changes fastest.
Arguments:
- train_factors: bfloat16 [16384, 2, 256, 128], P(('train', 'query')), may hold values from -6 to 6
- train_lengths: int32 [16384], P(('train', 'query')), may hold values from 64 to 256, as said below
- query_factors: bfloat16 [128, 2, 8192, 128], P('query', None, 'train'), may hold values from -6 to 6
- query_lengths: int32 [128], P('query'), may hold values from 4097 to 8192, as said below
- basis_out: float32 [2, 64, 64], replicated, may hold values from -0.75 to 0.75
- basis_in: float32 [2, 64, 64], replicated, may hold values from -0.75 to 0.75
- eigenvalues: float32 [2, 64, 64], replicated, may hold values from 0.1 to 10
Outputs:
- scores: float32 [16384, 128], P('train', 'query')
Inputs may be any that keep to these rules, and one draw needn't show every extreme that they name: `train_lengths`: each train document has 256 live tokens or fewer, and some document in every draw has exactly 256; some has exactly 64. `query_lengths`: each query document has more than half of its 8192 slots live; some document in every draw has all 8192, and some has exactly 4097.
All inputs are finite; a program needn't handle non-finite values.
Results may differ from a plain program's by a relative error of at most 0.0035.
Values may be sent and summed in bfloat16 or wider, within the bound.
A program may use at most 64 MiB of HBM per device.

v0:
```python
import math

import jax
import jax.numpy as jnp
from jax import lax
from jax.sharding import PartitionSpec as P


def outer_sums(factors, live_mask, rank_width, token_norm):
    gradients = factors[..., rank_width:] * live_mask[:, None, :, None]
    summed = jnp.einsum(
        "dltr,dlts->dlrs", gradients, factors[..., :rank_width], preferred_element_type=jnp.float32
    )
    return summed * token_norm


def rotate(summed, basis_out, basis_in, inv_root):
    half_turn = jnp.einsum("lra,dlrs->dlas", basis_out, summed, precision=lax.Precision.HIGHEST)
    rotated = jnp.einsum("dlas,lsb->dlab", half_turn, basis_in, precision=lax.Precision.HIGHEST)
    rotated = rotated * inv_root[None]
    return rotated.reshape(rotated.shape[0], -1)


def on_device(
    train_factors, train_lengths, query_factors, query_lengths, basis_out, basis_in, eigenvalues
):
    rank_width = basis_in.shape[1]
    layer_count = basis_in.shape[0]
    inv_root = 1.0 / jnp.sqrt(eigenvalues)
    score_norm = 1.0 / (rank_width * math.sqrt(layer_count))
    piece_len = query_factors.shape[2]
    query_slots = piece_len * lax.axis_size("train")
    positions = lax.axis_index("train") * piece_len + jnp.arange(piece_len, dtype=jnp.int32)
    query_live = (positions[None, :] < query_lengths[:, None]).astype(jnp.bfloat16)
    query_part = outer_sums(query_factors, query_live, rank_width, 1.0 / math.sqrt(query_slots))
    query_part = rotate(query_part, basis_out, basis_in, inv_root)
    train_slots = train_factors.shape[2]
    train_live = (
        jnp.arange(train_slots, dtype=jnp.int32)[None, :] < train_lengths[:, None]
    ).astype(jnp.bfloat16)
    train_sums = outer_sums(train_factors, train_live, rank_width, 1.0 / math.sqrt(train_slots))
    train_rotated = rotate(train_sums, basis_out, basis_in, inv_root).astype(jnp.bfloat16)
    query_rotated = lax.psum(query_part, "train").astype(jnp.bfloat16)
    product = lax.dot_general(
        lax.all_gather(train_rotated, "query", axis=0, tiled=True),
        query_rotated,
        (((1,), (1,)), ((), ())),
        preferred_element_type=jnp.float32,
    )
    return product * score_norm


def solution(mesh):
    return jax.shard_map(
        on_device,
        mesh=mesh,
        in_specs=(
            P(("train", "query"), None, None, None),
            P(("train", "query")),
            P("query", None, "train", None),
            P("query"),
            P(),
            P(),
            P(),
        ),
        out_specs=P("train", "query"),
        check_vma=False,
    )
```

profile of v0, /device:TPU:1, one launch (start us, length us, event | category | flops | bytes accessed | tf_op | source)
XLA Modules:
  0.0 182.9 jit_solution(12945319427930894530)
XLA Ops:
  6.5 0.0 copy-start
  6.5 0.0 all-gather.2.cloned.1.call-start
  6.5 0.8 fusion.30
  7.3 0.9 sqrt.3
  8.2 7.1 %fusion.11 = f32[32,2,64,64]{3,2,1,0:T(8,128)S(1)} fusion(bf16[32,2,256,128]{3,2,1,0:T(8,128)(2,1)} %param.7, bf16[32,256]{1,0:T(8,128)(2,1)S(1)} %fusion.30), kind=kOutput, calls=%fused_computation.10 | convolution fusion | flops 135528448 | bytes 9453568 | tf_op jit(solution)/shard_map/dltr,dlts->dlrs/dot_general | solution.py:11
  15.3 0.0 copy-done
  15.3 0.0 copy-start.1
  15.3 1.9 %fusion.6 = f32[2,32,64,64]{2,3,1,0:T(8,128)S(1)} fusion(f32[32,2,64,64]{3,2,1,0:T(8,128)S(1)} %fusion.11, f32[2,64,64]{2,1,0:T(8,128)S(1)} %copy-done), kind=kOutput, calls=%fused_computation.6 | convolution fusion | flops 201326592 | bytes 2129920 | tf_op jit(solution)/shard_map/lra,dlrs->dlas/dot_general | solution.py:18
  17.3 0.0 copy-done.1
  17.3 1.9 %fusion.16 = bf16[32,2,64,64]{3,2,0,1:T(8,128)(2,1)S(1)} fusion(f32[2,32,64,64]{2,3,1,0:T(8,128)S(1)} %fusion.6, f32[2,64,64]{2,1,0:T(8,128)S(1)} %sqrt.3, f32[2,64,64]{2,1,0:T(8,128)S(1)} %copy-done.1), kind=kOutput, calls=%fused_computation.11 | convolution fusion | flops 201850880 | bytes 1638400 | tf_op jit(solution)/shard_map/dlas,lsb->dlab/dot_general | solution.py:19
  19.2 0.0 copy-start.2
  19.3 0.0 copy-start.3
  19.3 0.1 copy.8
  19.4 1.7 convert_element_type.29
  21.0 0.0 all-gather.2.cloned.1.call-update
  21.1 0.0 copy-done.2
  21.1 0.1 compare_convert_fusion
  21.2 0.0 copy-done.3
  21.2 1.3 convolution_multiply_fusion
  22.4 0.6 convolution_bitcast_fusion
  23.1 0.6 fusion.19
  23.7 0.2 reshape.58
  23.9 114.0 %all-reduce.1 = bf16[8,8192]{1,0:T(8,128)(2,1)S(1)} all-reduce(f32[8,8192]{1,0:T(8,128)S(1)} %reshape.58), channel_id=1, replica_groups=mesh['train'=32,'query'=16] {'train'}, use_global_device_ids=true, to_apply=%region_0.0 | all-reduce | flops 65536 | bytes 393216 | tf_op jit(solution)/shard_map/psum | solution.py:43
  137.9 31.9 %all-gather.2.cloned.1.call-done = bf16[512,8192]{1,0:T(8,128)(2,1)} async-done(((bf16[32,8192]{1,0:T(8,128)(2,1)}), bf16[512,8192]{1,0:T(8,128)(2,1)}) %all-gather.2.cloned.1.call-update) | async-done | bytes 8388624 | tf_op jit(solution)/shard_map/all_gather | solution.py:45
  169.8 6.3 %convolution_multiply_fusion.2 = f32[512,8]{0,1:T(8,128)} fusion(bf16[512,8192]{1,0:T(8,128)(2,1)} %all-gather.2.cloned.1.call-done, bf16[8,8192]{1,0:T(8,128)(2,1)S(1)} %all-reduce.1), kind=kOutput, calls=%fused_computation.16 | convolution fusion | flops 67112960 | bytes 8536064 | tf_op jit(solution)/shard_map/dot_general | solution.py:44
  (2 shorter events, 0.0 us)
Async XLA Ops:
  6.5 8.8 %copy-start = (f32[2,64,64]{2,1,0:T(8,128)S(1)}, f32[2,64,64]{2,1,0:T(8,128)}, u32[]{:S(2)}) copy-start(f32[2,64,64]{2,1,0:T(8,128)} %param.11) | copy-start | bytes 98308
  6.5 163.2 %all-gather.2.cloned.1.call-start = ((), (), s32[]{:S(2)}) async-start(), calls=%async_computation | async-start | bytes 8912896 | tf_op jit(solution)/shard_map/all_gather | solution.py:45
  15.3 2.0 %copy-start.1 = (f32[2,64,64]{2,1,0:T(8,128)S(1)}, f32[2,64,64]{2,1,0:T(8,128)}, u32[]{:S(2)}) copy-start(f32[2,64,64]{2,1,0:T(8,128)} %param.12) | copy-start | bytes 98308
  19.2 1.8 %copy-start.2 = (s32[8]{0:T(128)S(1)}, s32[8]{0:T(128)}, u32[]{:S(2)}) copy-start(s32[8]{0:T(128)} %param.10) | copy-start | bytes 100
  19.3 1.9 %copy-start.3 = (bf16[8,2,256,128]{3,2,1,0:T(8,128)(2,1)S(1)}, bf16[8,2,256,128]{3,2,1,0:T(8,128)(2,1)}, u32[]{:S(2)}) copy-start(bf16[8,2,256,128]{3,2,1,0:T(8,128)(2,1)} %param.9) | copy-start | bytes 3145732
Sparse Core Ops, SparseCore 0:
  21.2 148.5 all-gather.1
where the time goes:
time: 183 us
  blocking collectives  114 us (62%)
  waiting for transfers between devices  31.9 us (17%)
  matrix products  19.7 us (11%)
  between operations  13.5 us (7%)
  local copies, waits for them, and re-layouts  2.87 us (2%)
    psum x1, blocking collectives, on_device(): query_rotated = lax.psum(query_part, 'train').astype(jnp.bfloat16)  114 us
    all_gather x1, waiting for transfers between devices, on_device(): lax.all_gather(train_rotated, 'query', axis=0, tiled=True)  31.9 us
    dot_general x2, matrix products, outer_sums(): jnp.einsum('dltr,dlts->dlrs', gradients, factors[..., :rank_width], prefe...  8.4 us
    dot_general x1, matrix products, on_device(): lax.dot_general(lax.all_gather(train_rotated, 'query', axis=0, tiled=True...  6.26 us
  transfers between devices with their start and end apart: 1, of which 1 were waited for; matrix products, arithmetic and copies ran while one was open for 2% of the time, Pallas kernels for 0%

commit v1 on v0

v1 whole, which is shorter than its diff:
```python
import functools
import math

import jax
import jax.numpy as jnp
from jax import lax
from jax.experimental import pallas as pl
from jax.experimental.pallas import tpu as pltpu
from jax.sharding import PartitionSpec as P

F32 = jnp.float32
BF16 = jnp.bfloat16
MESH = pl.DeviceIdType.MESH


def split(value):
    high = value.astype(BF16)
    return high, (value - high.astype(F32)).astype(BF16)


def mm(lhs, rhs):
    return jnp.dot(lhs, rhs, preferred_element_type=F32)


def kernel(
    nz, ny, score_norm, train_norm, query_norm,
    train_hbm, train_len, query_hbm, query_len, basis_out, basis_in, eigenvalues,
    out_ref,
    train_buf, query_buf, right_ref, left_ref, scale_ref,
    partial, sibling_part, pieces, gathered, rotated, score_send, score_recv,
    load_sem, query_sem, pair_sem, reduce_sem, plane_sem, ring_sem, ring_send_sem, sib_sem, score_sem,
):
    rank = basis_in.shape[1]
    lanes = 2 * rank
    train_docs = train_hbm.shape[0]
    query_docs = query_hbm.shape[0]
    slots = train_hbm.shape[2]
    pairs = nz * 2
    plane = ny * 4
    groups = ny * 2
    chunk = plane
    half = chunk // 2
    chunks = nz

    train = lax.axis_index("train")
    query = lax.axis_index("query")
    z = train // 4
    x_lo = (train // 2) % 2
    core = train % 2
    x_hi = query // ny
    y = query % ny
    pair = train // 2
    c = core * y + (1 - core) * z
    d = core * z + (1 - core) * y
    spot = d * 4 + x_lo * 2 + x_hi

    sibling = (train + 1 - 2 * core, query)

    def reduce_partner(j):
        other = (pair + j) % pairs
        return other, (other * 2 + core, query)

    def plane_partner(j):
        other = (spot + j) % plane
        od = other // 4
        oxl = (other // 2) % 2
        oxh = other % 2
        oz = core * od + (1 - core) * z
        oy = core * y + (1 - core) * od
        return oz * 4 + oxl * 2 + core, oxh * ny + oy

    def ring_partner(step):
        oc = (c + step + chunks) % chunks
        oz = core * z + (1 - core) * oc
        oy = core * oc + (1 - core) * y
        return oz * 4 + x_lo * 2 + core, x_hi * ny + oy

    def score_partner(j):
        other = (query + j) % groups
        return other, (train, other)

    load_query = pltpu.make_async_copy(query_hbm, query_buf, query_sem)
    load_query.start()
    loads = []
    parts = load_sem.shape[0]
    part_docs = train_docs // parts
    for i in range(parts):
        window = pl.ds(i * part_docs, part_docs)
        loads.append(pltpu.make_async_copy(train_hbm.at[window], train_buf.at[window], load_sem.at[i]))
        loads[-1].start()

    barrier = pltpu.get_barrier_semaphore()
    pl.semaphore_signal(barrier, inc=1, device_id=sibling, device_id_type=MESH)

    def greet_reduce(j, carry):
        pl.semaphore_signal(barrier, inc=1, device_id=reduce_partner(j)[1], device_id_type=MESH)
        return carry

    def greet_plane(j, carry):
        pl.semaphore_signal(barrier, inc=1, device_id=plane_partner(j), device_id_type=MESH)
        return carry

    def greet_score(j, carry):
        pl.semaphore_signal(barrier, inc=1, device_id=score_partner(j)[1], device_id_type=MESH)
        return carry

    lax.fori_loop(1, pairs, greet_reduce, 0)
    lax.fori_loop(1, plane, greet_plane, 0)
    lax.fori_loop(1, groups, greet_score, 0)
    for step in (1, -1):
        pl.semaphore_signal(barrier, inc=1, device_id=ring_partner(step), device_id_type=MESH)
    greetings = 1 + (pairs - 1) + (plane - 1) + (groups - 1) + 2

    zero = jnp.zeros((rank, rank), F32)
    block = jnp.concatenate(
        [
            jnp.concatenate([basis_in[0], zero], axis=1),
            jnp.concatenate([zero, basis_in[1]], axis=1),
        ],
        axis=0,
    )
    high, low = split(block)
    right_ref[...] = jnp.concatenate([high, high, low], axis=0)
    turned = jnp.concatenate([basis_out[0].T, basis_out[1].T], axis=0)
    high, low = split(turned)
    left_ref[...] = jnp.concatenate([high, high, low], axis=1)
    scale_ref[...] = 1.0 / jnp.sqrt(jnp.concatenate([eigenvalues[0], eigenvalues[1]], axis=1))

    lane = lax.broadcasted_iota(jnp.int32, (rank, lanes), 1)
    first_layer = lane < rank
    token = lax.broadcasted_iota(jnp.int32, (slots, lanes), 0)

    def outer(factors, live):
        mask = jnp.where(token < live, 1.0, 0.0).astype(BF16)
        sums = []
        for layer in range(2):
            tokens = factors[layer]
            masked = tokens * mask
            product = lax.dot_general(
                masked, tokens, (((0,), (0,)), ((), ())), preferred_element_type=F32
            )
            sums.append(product[rank:])
        return jnp.where(first_layer, sums[0], pltpu.roll(sums[1], rank, 1))

    def rotate(summed, norm):
        count = len(summed)
        high, low = split(jnp.concatenate(summed, axis=0))
        turned = mm(jnp.concatenate([high, low, high], axis=1), right_ref[...])
        high, low = split(turned)
        columns = []
        for i in range(count):
            rows = slice(i * rank, (i + 1) * rank)
            columns.append(jnp.concatenate([high[rows], low[rows], high[rows]], axis=0))
        product = mm(left_ref[...], jnp.concatenate(columns, axis=1))
        scale = scale_ref[...] * norm
        results = []
        for i in range(count):
            mine = product[:, i * lanes:(i + 1) * lanes]
            results.append(jnp.where(first_layer, mine[:rank], mine[rank:]) * scale)
        return results

    load_query.wait()
    query_batch = 4

    def query_step(step, carry):
        summed = []
        for i in range(query_batch):
            doc = step * query_batch + i
            summed.append(outer(query_buf[doc], query_len[doc] - train * slots))
        for i, value in enumerate(rotate(summed, query_norm)):
            partial[:, pl.ds(step * query_batch + i, 1), :] = value[:, None, :]
        return carry

    lax.fori_loop(0, query_docs // query_batch, query_step, 0)

    pl.semaphore_wait(barrier, greetings)
    half_rows = rank // 2
    pair_copy = pltpu.make_async_remote_copy(
        src_ref=partial.at[pl.ds((1 - core) * half_rows, half_rows)],
        dst_ref=sibling_part,
        send_sem=pair_sem.at[0],
        recv_sem=pair_sem.at[1],
        device_id=sibling,
        device_id_type=MESH,
    )
    pair_copy.start()

    train_batch = 4
    per_part = part_docs // train_batch

    def train_step(step, carry):
        summed = []
        for i in range(train_batch):
            doc = step * train_batch + i
            summed.append(outer(train_buf[doc], train_len[doc]))
        for i, value in enumerate(rotate(summed, train_norm)):
            rotated[:, pl.ds(step * train_batch + i, 1), :] = value[:, None, :]
        return carry

    def train_part(i):
        loads[i].wait()
        lax.fori_loop(i * per_part, (i + 1) * per_part, train_step, 0)

    pair_copy.wait()
    sibling_part[...] = sibling_part[...] + partial[pl.ds(core * half_rows, half_rows)]

    def send_reduce(j, carry):
        other, target = reduce_partner(j)
        pltpu.make_async_remote_copy(
            src_ref=sibling_part.at[pl.ds(other * 2, 2)],
            dst_ref=pieces.at[j],
            send_sem=reduce_sem.at[0],
            recv_sem=reduce_sem.at[1],
            device_id=target,
            device_id_type=MESH,
        ).start()
        return carry

    lax.fori_loop(1, pairs, send_reduce, 0)
    train_part(0)
    others = pieces.at[pl.ds(1, pairs - 1)]
    pltpu.make_async_copy(others, others, reduce_sem.at[1]).wait()
    total = sibling_part[pl.ds(pair * 2, 2)]
    for j in range(1, pairs):
        total = total + pieces[j]
    tile_rows = 2 * query_docs
    gathered[core, c * plane + spot] = total.reshape(tile_rows, lanes).astype(BF16)

    mine = gathered.at[core, c * plane + spot]

    def send_plane(j, carry):
        pltpu.make_async_remote_copy(
            src_ref=mine,
            dst_ref=mine,
            send_sem=plane_sem.at[0],
            recv_sem=plane_sem.at[1],
            device_id=plane_partner(j),
            device_id_type=MESH,
        ).start()
        return carry

    lax.fori_loop(1, plane, send_plane, 0)
    train_part(1)
    others = gathered.at[0, pl.ds(0, plane - 1)]
    pltpu.make_async_copy(others, others, plane_sem.at[1]).wait()

    steps = chunks // 2

    def window(origin, sub, count):
        return gathered.at[core, pl.ds(origin * chunk + sub * half, count)]

    def ring_copy(way, step, sub):
        origin = (c - way * (step - 1) + chunks) % chunks
        side = (1 - way) // 2
        return pltpu.make_async_remote_copy(
            src_ref=window(origin, sub, half),
            dst_ref=window(origin, sub, half),
            send_sem=ring_send_sem,
            recv_sem=ring_sem.at[side, step - 1, sub],
            device_id=ring_partner(way),
            device_id_type=MESH,
        )

    def sib_copy(origin, sub, count):
        return pltpu.make_async_remote_copy(
            src_ref=window(origin, sub, count),
            dst_ref=window(origin, sub, count),
            send_sem=sib_sem.at[0],
            recv_sem=sib_sem.at[1],
            device_id=sibling,
            device_id_type=MESH,
        )

    def wanted(way, step, sub):
        return step < steps or (step == steps and sub == (1 - way) // 2)

    for sub in range(2):
        for way in (1, -1):
            if wanted(way, 1, sub):
                ring_copy(way, 1, sub).start()
    sib_copy(c, 0, chunk).start()
    done = 2
    for step in range(1, steps + 1):
        if done < parts:
            train_part(done)
            done += 1
        for sub in range(2):
            for way in (1, -1):
                if not wanted(way, step, sub):
                    continue
                ring_copy(way, step, sub).wait_recv()
                if wanted(way, step + 1, sub):
                    ring_copy(way, step + 1, sub).start()
                sib_copy((c - way * step + chunks) % chunks, sub, half).start()
    for i in range(done, parts):
        train_part(i)
    whole = gathered.at[0]
    pltpu.make_async_copy(whole, whole, sib_sem.at[1]).wait()

    rows = groups * tile_rows

    total = jnp.zeros((rows, 2 * train_docs), F32)
    for side in range(2):
        for i in range(pairs):
            iz, ixl = i // 2, i % 2
            tiles = []
            for iy in range(ny):
                first = (iz * ny + iy if side == 0 else iy * nz + iz) * 4 + ixl * 2
                tiles.append(gathered[side, first:first + 2].reshape(2 * tile_rows, lanes))
            row = side * half_rows + 2 * i
            documents = rotated[row:row + 2].reshape(2 * train_docs, lanes).astype(BF16)
            total = total + lax.dot_general(
                jnp.concatenate(tiles, axis=0), documents, (((1,), (1,)), ((), ())), preferred_element_type=F32
            )
    total = total.reshape(groups, 2, query_docs, 2 * train_docs)
    scores = (total[:, 0, :, :train_docs] + total[:, 1, :, train_docs:]) * score_norm
    share = score_recv.shape[2] // train_docs
    wide = jnp.concatenate([scores] * share, axis=2)
    lane = lax.broadcasted_iota(jnp.int32, wide.shape, 2)
    place = query % share
    score_send[...] = jnp.where((lane >= place * train_docs) & (lane < (place + 1) * train_docs), wide, 0.0)

    def send_scores(j, carry):
        other, target = score_partner(j)
        pltpu.make_async_remote_copy(
            src_ref=score_send.at[(other % ny) * 2 + other // ny],
            dst_ref=score_recv.at[query],
            send_sem=score_sem.at[0],
            recv_sem=score_sem.at[1],
            device_id=target,
            device_id_type=MESH,
        ).start()
        return carry

    lax.fori_loop(1, groups, send_scores, 0)
    score_recv[query] = score_send[y * 2 + x_hi]

    pltpu.make_async_copy(others, others, plane_sem.at[0]).wait()
    others = pieces.at[pl.ds(1, pairs - 1)]
    pltpu.make_async_copy(others, others, reduce_sem.at[0]).wait()
    others = gathered.at[0, pl.ds(0, (chunks - 1) * chunk)]
    pltpu.make_async_copy(others, others, ring_send_sem).wait()
    pltpu.make_async_copy(whole, whole, sib_sem.at[0]).wait()

    others = score_recv.at[pl.ds(0, groups - 1)]
    pltpu.make_async_copy(others, others, score_sem.at[1]).wait()
    for i in range(groups // share):
        value = score_recv[i * share]
        for k in range(1, share):
            value = value + score_recv[i * share + k]
        out_ref[:, i * share * train_docs:(i + 1) * share * train_docs] = value
    pltpu.make_async_copy(others, others, score_sem.at[0]).wait()


def on_device(
    train_factors, train_lengths, query_factors, query_lengths, basis_out, basis_in, eigenvalues
):
    layer_count, rank, _ = basis_in.shape
    train_docs, _, slots, lanes = train_factors.shape
    query_docs = query_factors.shape[0]
    trains = lax.axis_size("train")
    groups = lax.axis_size("query")
    nz, ny = trains // 4, groups // 2
    pairs, plane = nz * 2, ny * 4
    tile_rows = 2 * query_docs
    share = min(groups, 128 // train_docs)
    score_norm = 1.0 / (rank * math.sqrt(layer_count))
    train_norm = 1.0 / math.sqrt(slots)
    query_norm = 1.0 / math.sqrt(slots * trains)
    vmem = pl.BlockSpec(memory_space=pltpu.VMEM)
    smem = pl.BlockSpec(memory_space=pltpu.SMEM)
    hbm = pl.BlockSpec(memory_space=pl.ANY)
    dma = pltpu.SemaphoreType.DMA
    scores = pl.pallas_call(
        functools.partial(kernel, nz, ny, score_norm, train_norm, query_norm),
        out_shape=jax.ShapeDtypeStruct((query_docs, groups * train_docs), F32),
        in_specs=[hbm, smem, hbm, smem, vmem, vmem, vmem],
        out_specs=vmem,
        scratch_shapes=[
            pltpu.VMEM(train_factors.shape, BF16),
            pltpu.VMEM(query_factors.shape, BF16),
            pltpu.VMEM((3 * lanes, lanes), BF16),
            pltpu.VMEM((lanes, 3 * rank), BF16),
            pltpu.VMEM((rank, lanes), F32),
            pltpu.VMEM((rank, query_docs, lanes), F32),
            pltpu.VMEM((rank // 2, query_docs, lanes), F32),
            pltpu.VMEM((pairs, 2, query_docs, lanes), F32),
            pltpu.VMEM((2, nz * plane, tile_rows, lanes), BF16),
            pltpu.VMEM((rank, train_docs, lanes), F32),
            pltpu.VMEM((groups, query_docs, share * train_docs), F32),
            pltpu.VMEM((groups, query_docs, share * train_docs), F32),
            dma((4,)),
            dma,
            dma((2,)),
            dma((2,)),
            dma((2,)),
            dma((2, nz // 2, 2)),
            dma,
            dma((2,)),
            dma((2,)),
        ],
        compiler_params=pltpu.CompilerParams(
            collective_id=0, has_side_effects=True, vmem_limit_bytes=40 * 1024 * 1024
        ),
        cost_estimate=pl.CostEstimate(flops=400_000_000, bytes_accessed=6_000_000, transcendentals=0),
    )(
        train_factors, train_lengths, query_factors, query_lengths, basis_out, basis_in, eigenvalues
    )
    return scores.T


def solution(mesh):
    return jax.shard_map(
        on_device,
        mesh=mesh,
        in_specs=(
            P(("train", "query"), None, None, None),
            P(("train", "query")),
            P("query", None, "train", None),
            P("query"),
            P(),
            P(),
            P(),
        ),
        out_specs=P("train", "query"),
        check_vma=False,
    )
```

time: 183 us -> 63.7 us (0.35)
  blocking collectives: 114 us -> 0 us
  Pallas kernels: 0 us -> 55.5 us
  waiting for transfers between devices: 31.9 us -> 0 us
  matrix products: 19.7 us -> 0 us
  between operations: 13.5 us -> 0.02 us
  local copies, waits for them, and re-layouts: 2.87 us -> 7.85 us
    psum x1 -> x0, blocking collectives: 114 us -> none  [on_device(): query_rotated = lax.psum(query_part, 'train').astype(jnp.bfloat16)]
    pallas_call x0 -> x1, Pallas kernels: none -> 55.5 us  [on_device(): pl.pallas_call(functools.partial(kernel, nz, ny, score_norm, train_norm,...]
    all_gather x1 -> x0, waiting for transfers between devices: 31.9 us -> none  [on_device(): lax.all_gather(train_rotated, 'query', axis=0, tiled=True)]
    dot_general x7 -> x0, matrix products: 19.7 us -> none  [the longest x2 8.4 us: outer_sums(): jnp.einsum('dltr,dlts->dlrs', gradients, factors[..., :rank_width], prefe...]
    unnamed x8 -> x15, local copies, waits for them, and re-layouts: 0.02 us -> 7.85 us
  transfers between devices with their start and end apart: 1 -> 0, of which waited for: 1 -> 0; matrix products, arithmetic and copies ran while one was open for 2% -> 0% of each run, Pallas kernels for 0% -> 0%
where the time goes in v1:
time: 63.7 us; the launch traced here: 63.3 us
  Pallas kernels  55.5 us (87%)
  local copies, waits for them, and re-layouts  7.85 us (12%)
    pallas_call x1, Pallas kernels, on_device(): pl.pallas_call(functools.partial(kernel, nz, ny, score_norm, train_norm,...  55.5 us
    unnamed x15, local copies, waits for them, and re-layouts  7.85 us

profile of v1, /device:TPU:1, one launch (start us, length us, event | category | flops | bytes accessed | tf_op | source)
XLA Modules:
  0.0 63.3 jit_solution(14452792964057745907)
XLA Ops:
  0.0 0.0 copy-start
  0.0 2.2 %copy-done = bf16[32,2,256,128]{3,2,1,0:T(8,128)(2,1)S(1)} copy-done((bf16[32,2,256,128]{3,2,1,0:T(8,128)(2,1)S(1)}, bf16[32,2,256,128]{3,2,1,0:T(8,128)(2,1)}, u32[]{:S(2)}) %copy-start) | copy-done | bytes 4194328
  2.2 0.0 copy-start.1
  2.2 1.2 %copy-done.1 = bf16[8,2,256,128]{3,2,1,0:T(8,128)(2,1)S(1)} copy-done((bf16[8,2,256,128]{3,2,1,0:T(8,128)(2,1)S(1)}, bf16[8,2,256,128]{3,2,1,0:T(8,128)(2,1)}, u32[]{:S(2)}) %copy-start.1) | copy-done | bytes 1048600
  3.4 0.0 copy-start.2
  3.4 0.8 %copy-done.2 = f32[2,64,64]{2,1,0:T(8,128)S(1)} copy-done((f32[2,64,64]{2,1,0:T(8,128)S(1)}, f32[2,64,64]{2,1,0:T(8,128)}, u32[]{:S(2)}) %copy-start.2) | copy-done | bytes 32792
  4.3 0.0 copy-start.3
  4.3 0.8 %copy-done.3 = f32[2,64,64]{2,1,0:T(8,128)S(1)} copy-done((f32[2,64,64]{2,1,0:T(8,128)S(1)}, f32[2,64,64]{2,1,0:T(8,128)}, u32[]{:S(2)}) %copy-start.3) | copy-done | bytes 32792
  5.1 0.0 copy-start.4
  5.1 0.8 %copy-done.4 = f32[2,64,64]{2,1,0:T(8,128)S(1)} copy-done((f32[2,64,64]{2,1,0:T(8,128)S(1)}, f32[2,64,64]{2,1,0:T(8,128)}, u32[]{:S(2)}) %copy-start.4) | copy-done | bytes 32792
  5.9 0.0 copy-start.5
  5.9 0.7 %copy-done.5 = s32[32]{0:T(128)S(1)} copy-done((s32[32]{0:T(128)S(1)}, s32[32]{0:T(128)}, u32[]{:S(2)}) %copy-start.5) | copy-done | bytes 152
  6.6 0.0 copy-start.6
  6.6 0.7 %copy-done.6 = s32[8]{0:T(128)S(1)} copy-done((s32[8]{0:T(128)S(1)}, s32[8]{0:T(128)}, u32[]{:S(2)}) %copy-start.6) | copy-done | bytes 56
  7.2 55.5 %shard_map.73 = f32[8,512]{1,0:T(8,128)S(1)} custom-call(bf16[32,2,256,128]{3,2,1,0:T(8,128)(2,1)S(1)} %copy-done, s32[32]{0:T(128)S(1)} %copy-done.5, bf16[8,2,256,128]{3,2,1,0:T(8,128)(2,1)S(1)} %copy-done.1, s32[8]{0:T(128)S(1)} %copy-done.6, f32[2,64,64]{2,1,0:T(8,128)S(1)} %copy-done.2, f32[2,64,64]{2,1,0:T(8,128)S(1)} %copy-done.3, ...), custom_call_target="tpu_custom_call" | custom-call | flops 400000000 | bytes 6000000 | tf_op jit(solution)/shard_map/pallas_call | solution.py:374
  62.7 0.6 copy.9
Async XLA Ops:
  0.0 2.2 %copy-start = (bf16[32,2,256,128]{3,2,1,0:T(8,128)(2,1)S(1)}, bf16[32,2,256,128]{3,2,1,0:T(8,128)(2,1)}, u32[]{:S(2)}) copy-start(bf16[32,2,256,128]{3,2,1,0:T(8,128)(2,1)} %train_hbm.1) | copy-start | bytes 12582916
  2.2 1.2 %copy-start.1 = (bf16[8,2,256,128]{3,2,1,0:T(8,128)(2,1)S(1)}, bf16[8,2,256,128]{3,2,1,0:T(8,128)(2,1)}, u32[]{:S(2)}) copy-start(bf16[8,2,256,128]{3,2,1,0:T(8,128)(2,1)} %query_hbm.1) | copy-start | bytes 3145732
  3.4 0.8 %copy-start.2 = (f32[2,64,64]{2,1,0:T(8,128)S(1)}, f32[2,64,64]{2,1,0:T(8,128)}, u32[]{:S(2)}) copy-start(f32[2,64,64]{2,1,0:T(8,128)} %basis_out.1) | copy-start | bytes 98308
  4.3 0.8 %copy-start.3 = (f32[2,64,64]{2,1,0:T(8,128)S(1)}, f32[2,64,64]{2,1,0:T(8,128)}, u32[]{:S(2)}) copy-start(f32[2,64,64]{2,1,0:T(8,128)} %basis_in.1) | copy-start | bytes 98308
  5.1 0.8 %copy-start.4 = (f32[2,64,64]{2,1,0:T(8,128)S(1)}, f32[2,64,64]{2,1,0:T(8,128)}, u32[]{:S(2)}) copy-start(f32[2,64,64]{2,1,0:T(8,128)} %eigenvalues.1) | copy-start | bytes 98308
  5.9 0.7 %copy-start.5 = (s32[32]{0:T(128)S(1)}, s32[32]{0:T(128)}, u32[]{:S(2)}) copy-start(s32[32]{0:T(128)} %train_len.1) | copy-start | bytes 388
  6.6 0.7 %copy-start.6 = (s32[8]{0:T(128)S(1)}, s32[8]{0:T(128)}, u32[]{:S(2)}) copy-start(s32[8]{0:T(128)} %query_len.1) | copy-start | bytes 100

commit v2 on v1

v2 whole, which is shorter than its diff:
```python
import functools
import math

import jax
import jax.numpy as jnp
from jax import lax
from jax.experimental import pallas as pl
from jax.experimental.pallas import tpu as pltpu
from jax.sharding import PartitionSpec as P

F32 = jnp.float32
BF16 = jnp.bfloat16
MESH = pl.DeviceIdType.MESH


def split(value):
    high = value.astype(BF16)
    return high, (value - high.astype(F32)).astype(BF16)


def mm(lhs, rhs):
    return jnp.dot(lhs, rhs, preferred_element_type=F32)


def kernel(
    nz, ny, score_norm, train_norm, query_norm,
    train_hbm, train_len_hbm, query_hbm, query_len_hbm, basis_out_hbm, basis_in_hbm, eigenvalues_hbm,
    out_ref,
    train_buf, train_len, query_buf, query_len, basis_out, basis_in, eigenvalues,
    right_ref, left_ref, scale_ref,
    partial, sibling_part, pieces, gathered, rotated, rows_own, rows_all, score_send, score_recv,
    load_sem, query_sem, small_sem, pair_sem, reduce_sem, plane_sem, sib_sem, rows_sem, score_sem,
):
    rank = basis_in.shape[1]
    lanes = 2 * rank
    train_docs = train_hbm.shape[0]
    query_docs = query_hbm.shape[0]
    slots = train_hbm.shape[2]
    slab = rank // ny
    groups = ny * 2
    plane = nz * 4
    tile_rows = 2 * query_docs

    train = lax.axis_index("train")
    query = lax.axis_index("query")
    z = train // 4
    x_lo = (train // 2) % 2
    core = train % 2
    x_hi = query // ny
    y = query % ny
    spot = z * 4 + x_hi * 2 + x_lo
    tile_group = x_hi * ny + z

    def device(dz, dxl, dxh, dy):
        return dz * 4 + dxl * 2 + core, dxh * ny + dy

    sibling = (train + 1 - 2 * core, query)

    def plane_partner(j):
        other = (spot + j) % plane
        return device(other // 4, other % 2, (other // 2) % 2, y)

    def score_partner(j):
        other = (query + j) % groups
        return other, (train, other)

    load_query = pltpu.make_async_copy(query_hbm, query_buf, query_sem)
    load_query.start()
    small = [
        pltpu.make_async_copy(src, dst, small_sem.at[i])
        for i, (src, dst) in enumerate(
            [
                (query_len_hbm, query_len),
                (basis_in_hbm, basis_in),
                (basis_out_hbm, basis_out),
                (eigenvalues_hbm, eigenvalues),
                (train_len_hbm, train_len),
            ]
        )
    ]
    for copy in small:
        copy.start()
    parts = load_sem.shape[0]
    part_docs = train_docs // parts
    loads = []
    for i in range(parts):
        window = pl.ds(i * part_docs, part_docs)
        loads.append(pltpu.make_async_copy(train_hbm.at[window], train_buf.at[window], load_sem.at[i]))
        loads[-1].start()

    barrier = pltpu.get_barrier_semaphore()

    def greet(target):
        pl.semaphore_signal(barrier, inc=1, device_id=target, device_id_type=MESH)

    greet(sibling)

    def greet_reduce(j, carry):
        source = device(j // 2, j % 2, x_hi, z)
        own = (source[0] == train) & (source[1] == query)
        greet((source[0] + jnp.where(own, 1 - 2 * core, 0), source[1]))
        return carry

    def greet_plane(j, carry):
        greet(plane_partner(j))
        return carry

    def greet_score(j, carry):
        greet(score_partner(j)[1])
        return carry

    lax.fori_loop(0, nz * 2, greet_reduce, 0)
    lax.fori_loop(1, plane, greet_plane, 0)
    lax.fori_loop(1, groups, greet_score, 0)
    greetings = 1 + nz * 2 + (plane - 1) + (groups - 1)

    for copy in small:
        copy.wait()
    zero = jnp.zeros((rank, rank), F32)
    block = jnp.concatenate(
        [
            jnp.concatenate([basis_in[0], zero], axis=1),
            jnp.concatenate([zero, basis_in[1]], axis=1),
        ],
        axis=0,
    )
    high, low = split(block)
    right_ref[...] = jnp.concatenate([high, high, low], axis=0)
    turned = jnp.concatenate([basis_out[0].T, basis_out[1].T], axis=0)
    high, low = split(turned)
    left_ref[...] = jnp.concatenate([high, high, low], axis=1)
    scale_ref[...] = 1.0 / jnp.sqrt(jnp.concatenate([eigenvalues[0], eigenvalues[1]], axis=1))

    lane = lax.broadcasted_iota(jnp.int32, (rank, lanes), 1)
    first_layer = lane < rank
    token = lax.broadcasted_iota(jnp.int32, (slots, lanes), 0)

    def outer(factors, live):
        mask = jnp.where(token < live, 1.0, 0.0).astype(BF16)
        sums = []
        for layer in range(2):
            tokens = factors[layer]
            masked = tokens * mask
            product = lax.dot_general(
                masked, tokens, (((0,), (0,)), ((), ())), preferred_element_type=F32
            )
            sums.append(product[rank:])
        return jnp.where(first_layer, sums[0], pltpu.roll(sums[1], rank, 1))

    def rotate(summed, norm):
        count = len(summed)
        high, low = split(jnp.concatenate(summed, axis=0))
        turned = mm(jnp.concatenate([high, low, high], axis=1), right_ref[...])
        high, low = split(turned)
        columns = []
        for i in range(count):
            rows = slice(i * rank, (i + 1) * rank)
            columns.append(jnp.concatenate([high[rows], low[rows], high[rows]], axis=0))
        product = mm(left_ref[...], jnp.concatenate(columns, axis=1))
        scale = scale_ref[...] * norm
        results = []
        for i in range(count):
            mine = product[:, i * lanes:(i + 1) * lanes]
            results.append(jnp.where(first_layer, mine[:rank], mine[rank:]) * scale)
        return results

    load_query.wait()
    query_batch = 4

    def query_step(step, carry):
        summed = []
        for i in range(query_batch):
            doc = step * query_batch + i
            summed.append(outer(query_buf[doc], query_len[doc] - train * slots))
        for i, value in enumerate(rotate(summed, query_norm)):
            partial[:, :, :, pl.ds(step * query_batch + i, 1), :] = value.reshape(ny, 2, slab // 2, 1, lanes)
        return carry

    lax.fori_loop(0, query_docs // query_batch, query_step, 0)

    pl.semaphore_wait(barrier, greetings)
    pair_copy = pltpu.make_async_remote_copy(
        src_ref=partial.at[:, 1 - core],
        dst_ref=sibling_part,
        send_sem=pair_sem.at[0],
        recv_sem=pair_sem.at[1],
        device_id=sibling,
        device_id_type=MESH,
    )
    pair_copy.start()

    train_batch = 4
    per_part = part_docs // train_batch

    def train_step(step, carry):
        summed = []
        for i in range(train_batch):
            doc = step * train_batch + i
            summed.append(outer(train_buf[doc], train_len[doc]))
        for i, value in enumerate(rotate(summed, train_norm)):
            rotated[:, pl.ds(step * train_batch + i, 1), :] = value[:, None, :]
        return carry

    def train_part(i):
        loads[i].wait()
        lax.fori_loop(i * per_part, (i + 1) * per_part, train_step, 0)

    batches = rows_own.shape[1]
    batch_docs = train_docs // batches

    def send_rows(i):
        rows_own[:, i] = rotated[:, i * batch_docs:(i + 1) * batch_docs, :].astype(BF16)

        def send(j, carry):
            other = (y + j) % ny
            pltpu.make_async_remote_copy(
                src_ref=rows_own.at[pl.ds(other * slab, slab), i],
                dst_ref=rows_all.at[:, y, i],
                send_sem=rows_sem.at[0],
                recv_sem=rows_sem.at[1],
                device_id=device(z, x_lo, x_hi, other),
                device_id_type=MESH,
            ).start()
            return carry

        lax.fori_loop(1, ny, send, 0)
        rows_all[:, y, i] = rows_own[pl.ds(y * slab, slab), i]

    pair_copy.wait()
    sibling_part[...] = sibling_part[...] + partial[:, core]

    def send_reduce(j, carry):
        s, half = j // 2, j % 2
        target = device(y, half, x_hi, s)
        src = sibling_part.at[s, pl.ds(half * 2, 2)]
        dst = pieces.at[z * 2 + x_lo]

        @pl.when((target[0] == train) & (target[1] == query))
        def _():
            pltpu.make_async_copy(src, dst, reduce_sem.at[1]).start()

        @pl.when((target[0] != train) | (target[1] != query))
        def _():
            pltpu.make_async_remote_copy(
                src_ref=src,
                dst_ref=dst,
                send_sem=reduce_sem.at[0],
                recv_sem=reduce_sem.at[1],
                device_id=target,
                device_id_type=MESH,
            ).start()

        return carry

    lax.fori_loop(0, ny * 2, send_reduce, 0)
    train_part(0)
    train_part(1)
    send_rows(0)
    pltpu.make_async_copy(pieces, pieces, reduce_sem.at[1]).wait()
    total = pieces[0]
    for j in range(1, nz * 2):
        total = total + pieces[j]
    gathered[core, x_lo * groups + tile_group] = total.reshape(tile_rows, lanes).astype(BF16)

    mine = gathered.at[core, x_lo * groups + tile_group]

    def send_plane(j, carry):
        pltpu.make_async_remote_copy(
            src_ref=mine,
            dst_ref=mine,
            send_sem=plane_sem.at[0],
            recv_sem=plane_sem.at[1],
            device_id=plane_partner(j),
            device_id_type=MESH,
        ).start()
        return carry

    lax.fori_loop(1, plane, send_plane, 0)
    train_part(2)
    train_part(3)
    send_rows(1)
    others = gathered.at[0, pl.ds(0, plane - 1)]
    pltpu.make_async_copy(others, others, plane_sem.at[1]).wait()

    sib_copy = pltpu.make_async_remote_copy(
        src_ref=gathered.at[core],
        dst_ref=gathered.at[core],
        send_sem=sib_sem.at[0],
        recv_sem=sib_sem.at[1],
        device_id=sibling,
        device_id_type=MESH,
    )
    sib_copy.start()
    received = rows_all.at[:, pl.ds(0, ny - 1)]
    pltpu.make_async_copy(received, received, rows_sem.at[1]).wait()

    ring_docs = ny * train_docs

    def product(side):
        result = None
        for xl in range(2):
            queries = gathered[side, pl.ds(xl * groups, groups)].reshape(groups * tile_rows, lanes)
            documents = rows_all[pl.ds(side * (slab // 2) + xl * 2, 2)].reshape(2 * ring_docs, lanes)
            term = lax.dot_general(
                queries, documents, (((1,), (1,)), ((), ())), preferred_element_type=F32
            )
            result = term if result is None else result + term
        result = result.reshape(groups, 2, query_docs, 2 * ring_docs)
        return (result[:, 0, :, :ring_docs] + result[:, 1, :, ring_docs:]) * score_norm

    first = product(core)
    sib_copy.wait_recv()
    score_send[...] = first + product(1 - core)

    def send_scores(j, carry):
        other, target = score_partner(j)
        pltpu.make_async_remote_copy(
            src_ref=score_send.at[other],
            dst_ref=score_recv.at[query],
            send_sem=score_sem.at[0],
            recv_sem=score_sem.at[1],
            device_id=target,
            device_id_type=MESH,
        ).start()
        return carry

    lax.fori_loop(1, groups, send_scores, 0)
    score_recv[query] = score_send[query]

    sib_copy.wait_send()
    pltpu.make_async_copy(others, others, plane_sem.at[0]).wait()
    pltpu.make_async_copy(received, received, rows_sem.at[0]).wait()
    own_tile = y == z
    sent = pieces.at[pl.ds(0, nz * 2 - 1)]

    @pl.when(own_tile)
    def _():
        pltpu.make_async_copy(sent, sent, reduce_sem.at[0]).wait()

    @pl.when(jnp.logical_not(own_tile))
    def _():
        pltpu.make_async_copy(pieces, pieces, reduce_sem.at[0]).wait()

    blocks = score_recv.at[pl.ds(0, groups - 1)]
    pltpu.make_async_copy(blocks, blocks, score_sem.at[1]).wait()
    for side in range(2):
        value = score_recv[side * ny]
        for k in range(1, ny):
            value = value + score_recv[side * ny + k]
        out_ref[:, side * ring_docs:(side + 1) * ring_docs] = value
    pltpu.make_async_copy(blocks, blocks, score_sem.at[0]).wait()


def on_device(
    train_factors, train_lengths, query_factors, query_lengths, basis_out, basis_in, eigenvalues
):
    layer_count, rank, _ = basis_in.shape
    train_docs, _, slots, lanes = train_factors.shape
    query_docs = query_factors.shape[0]
    trains = lax.axis_size("train")
    groups = lax.axis_size("query")
    nz, ny = trains // 4, groups // 2
    slab = rank // ny
    tile_rows = 2 * query_docs
    batches = 2
    score_norm = 1.0 / (rank * math.sqrt(layer_count))
    train_norm = 1.0 / math.sqrt(slots)
    query_norm = 1.0 / math.sqrt(slots * trains)
    vmem = pl.BlockSpec(memory_space=pltpu.VMEM)
    hbm = pl.BlockSpec(memory_space=pltpu.HBM)
    dma = pltpu.SemaphoreType.DMA
    scores = pl.pallas_call(
        functools.partial(kernel, nz, ny, score_norm, train_norm, query_norm),
        out_shape=jax.ShapeDtypeStruct((query_docs, groups * train_docs), F32),
        in_specs=[hbm] * 7,
        out_specs=vmem,
        scratch_shapes=[
            pltpu.VMEM(train_factors.shape, BF16),
            pltpu.SMEM(train_lengths.shape, jnp.int32),
            pltpu.VMEM(query_factors.shape, BF16),
            pltpu.SMEM(query_lengths.shape, jnp.int32),
            pltpu.VMEM(basis_out.shape, F32),
            pltpu.VMEM(basis_in.shape, F32),
            pltpu.VMEM(eigenvalues.shape, F32),
            pltpu.VMEM((3 * lanes, lanes), BF16),
            pltpu.VMEM((lanes, 3 * rank), BF16),
            pltpu.VMEM((rank, lanes), F32),
            pltpu.VMEM((ny, 2, slab // 2, query_docs, lanes), F32),
            pltpu.VMEM((ny, slab // 2, query_docs, lanes), F32),
            pltpu.VMEM((nz * 2, 2, query_docs, lanes), F32),
            pltpu.VMEM((2, 2 * groups, tile_rows, lanes), BF16),
            pltpu.VMEM((rank, train_docs, lanes), F32),
            pltpu.VMEM((rank, batches, train_docs // batches, lanes), BF16),
            pltpu.VMEM((slab, ny, batches, train_docs // batches, lanes), BF16),
            pltpu.VMEM((groups, query_docs, ny * train_docs), F32),
            pltpu.VMEM((groups, query_docs, ny * train_docs), F32),
            dma((4,)),
            dma,
            dma((5,)),
            dma((2,)),
            dma((2,)),
            dma((2,)),
            dma((2,)),
            dma((2,)),
            dma((2,)),
        ],
        compiler_params=pltpu.CompilerParams(
            collective_id=0, has_side_effects=True, vmem_limit_bytes=64 * 1024 * 1024
        ),
        cost_estimate=pl.CostEstimate(flops=400_000_000, bytes_accessed=6_000_000, transcendentals=0),
    )(
        train_factors, train_lengths, query_factors, query_lengths, basis_out, basis_in, eigenvalues
    )
    return scores.T


def solution(mesh):
    return jax.shard_map(
        on_device,
        mesh=mesh,
        in_specs=(
            P(("train", "query"), None, None, None),
            P(("train", "query")),
            P("query", None, "train", None),
            P("query"),
            P(),
            P(),
            P(),
        ),
        out_specs=P("train", "query"),
        check_vma=False,
    )
```

time: 63.7 us -> 46.6 us (0.73)
  the two profiles are of different devices: /device:TPU:1 before, /device:TPU:8 now
where the time goes in v2:
time: 46.6 us; the launch traced here: 46.4 us
  Pallas kernels  45.1 us (97%)
  local copies, waits for them, and re-layouts  1.32 us (3%)
    pallas_call x1, Pallas kernels, on_device(): pl.pallas_call(functools.partial(kernel, nz, ny, score_norm, train_norm,...  45.1 us
    unnamed x1, local copies, waits for them, and re-layouts  1.32 us

profile of v2, /device:TPU:8, one launch (start us, length us, event | category | flops | bytes accessed | tf_op | source)
XLA Modules:
  0.0 46.4 jit_solution(14812293719710928215)
XLA Ops:
  0.0 45.1 %shard_map.73 = f32[8,512]{1,0:T(8,128)} custom-call(bf16[32,2,256,128]{3,2,1,0:T(8,128)(2,1)} %train_hbm.1, s32[32]{0:T(128)} %train_len_hbm.1, bf16[8,2,256,128]{3,2,1,0:T(8,128)(2,1)} %query_hbm.1, s32[8]{0:T(128)} %query_len_hbm.1, f32[2,64,64]{2,1,0:T(8,128)} %basis_out_hbm.1, f32[2,64,64]{2,1,0:T(8,128)} %basis_in_hbm.1, f32[2,64,64]{2,1,0:T(8,128)} %eigenvalues_hbm.1), custom_call_target="tpu_custom_call" | custom-call | flops 400000000 | bytes 6000000 | tf_op jit(solution)/shard_map/pallas_call | solution.py:372
  45.1 1.3 %copy.9 = f32[512,8]{0,1:T(8,128)} copy(f32[512,8]{0,1:T(8,128)} %bitcast.1) | data formatting | bytes 32768

commit v3 on v2

--- a/solution.py
+++ b/solution.py
@@ -48,21 +48,30 @@
     core = train % 2
     x_hi = query // ny
     y = query % ny
-    spot = z * 4 + x_hi * 2 + x_lo
-    tile_group = x_hi * ny + z
+    z_at = [lax.rem(z + k, nz) for k in range(nz)]
+    y_at = [lax.rem(y + k, ny) for k in range(ny)]
+    x_at = [(x_lo, x_hi), (1 - x_lo, x_hi), (x_lo, 1 - x_hi), (1 - x_lo, 1 - x_hi)]
+
+    def hops(k, size):
+        return min(k, size - k)
+
+    plane_steps = [(k, m) for k in range(nz) for m in range(4) if k or m]
+    plane_steps.sort(key=lambda step: -hops(step[0], nz) - (0, 1, 2, 1)[step[1]])
+    score_steps = [(k, m) for k in range(ny) for m in range(2) if k or m]
+    score_steps.sort(key=lambda step: -hops(step[0], ny) - 2 * step[1])
+    ring_steps = sorted(range(1, ny), key=lambda k: -hops(k, ny))
 
     def device(dz, dxl, dxh, dy):
         return dz * 4 + dxl * 2 + core, dxh * ny + dy
 
     sibling = (train + 1 - 2 * core, query)
 
-    def plane_partner(j):
-        other = (spot + j) % plane
-        return device(other // 4, other % 2, (other // 2) % 2, y)
-
-    def score_partner(j):
-        other = (query + j) % groups
-        return other, (train, other)
+    def plane_partner(k, m):
+        return device(z_at[k], x_at[m][0], x_at[m][1], y)
+
+    def score_partner(k, m):
+        dxh = 1 - x_hi if m else x_hi
+        return dxh, y_at[k], (train, dxh * ny + y_at[k])
 
     load_query = pltpu.make_async_copy(query_hbm, query_buf, query_sem)
     load_query.start()
@@ -93,26 +102,19 @@
     def greet(target):
         pl.semaphore_signal(barrier, inc=1, device_id=target, device_id_type=MESH)
 
+    own_tile = y == z
+    for k in range(nz):
+        for half in range(2):
+            source, group = device(z_at[k], half, x_hi, z)
+            if k == 0:
+                source = source + jnp.where(own_tile & (x_lo == half), 1 - 2 * core, 0)
+            greet((source, group))
+    for k, m in plane_steps:
+        greet(plane_partner(k, m))
+    for k, m in score_steps:
+        greet(score_partner(k, m)[2])
     greet(sibling)
-
-    def greet_reduce(j, carry):
-        source = device(j // 2, j % 2, x_hi, z)
-        own = (source[0] == train) & (source[1] == query)
-        greet((source[0] + jnp.where(own, 1 - 2 * core, 0), source[1]))
-        return carry
-
-    def greet_plane(j, carry):
-        greet(plane_partner(j))
-        return carry
-
-    def greet_score(j, carry):
-        greet(score_partner(j)[1])
-        return carry
-
-    lax.fori_loop(0, nz * 2, greet_reduce, 0)
-    lax.fori_loop(1, plane, greet_plane, 0)
-    lax.fori_loop(1, groups, greet_score, 0)
-    greetings = 1 + nz * 2 + (plane - 1) + (groups - 1)
+    greetings = 1 + nz * 2 + len(plane_steps) + len(score_steps)
 
     for copy in small:
         copy.wait()
@@ -211,86 +213,91 @@
     def send_rows(i):
         rows_own[:, i] = rotated[:, i * batch_docs:(i + 1) * batch_docs, :].astype(BF16)
 
-        def send(j, carry):
-            other = (y + j) % ny
+        for k in ring_steps:
             pltpu.make_async_remote_copy(
-                src_ref=rows_own.at[pl.ds(other * slab, slab), i],
+                src_ref=rows_own.at[pl.ds(y_at[k] * slab, slab), i],
                 dst_ref=rows_all.at[:, y, i],
                 send_sem=rows_sem.at[0],
                 recv_sem=rows_sem.at[1],
-                device_id=device(z, x_lo, x_hi, other),
+                device_id=device(z, x_lo, x_hi, y_at[k]),
                 device_id_type=MESH,
             ).start()
-            return carry
-
-        lax.fori_loop(1, ny, send, 0)
         rows_all[:, y, i] = rows_own[pl.ds(y * slab, slab), i]
 
     pair_copy.wait()
     sibling_part[...] = sibling_part[...] + partial[:, core]
 
-    def send_reduce(j, carry):
-        s, half = j // 2, j % 2
-        target = device(y, half, x_hi, s)
-        src = sibling_part.at[s, pl.ds(half * 2, 2)]
-        dst = pieces.at[z * 2 + x_lo]
-
-        @pl.when((target[0] == train) & (target[1] == query))
-        def _():
+    def send_reduce(s, half, target):
+        pltpu.make_async_remote_copy(
+            src_ref=sibling_part.at[s, pl.ds(half * 2, 2)],
+            dst_ref=pieces.at[z * 2 + x_lo],
+            send_sem=reduce_sem.at[0],
+            recv_sem=reduce_sem.at[1],
+            device_id=target,
+            device_id_type=MESH,
+        ).start()
+
+    for k in ring_steps:
+        for half in range(2):
+            send_reduce(y_at[k], half, device(y, half, x_hi, y_at[k]))
+    for half in range(2):
+        itself = own_tile & (x_lo == half)
+
+        @pl.when(itself)
+        def _(half=half):
+            src, dst = sibling_part.at[y, pl.ds(half * 2, 2)], pieces.at[z * 2 + x_lo]
             pltpu.make_async_copy(src, dst, reduce_sem.at[1]).start()
 
-        @pl.when((target[0] != train) | (target[1] != query))
-        def _():
-            pltpu.make_async_remote_copy(
-                src_ref=src,
-                dst_ref=dst,
-                send_sem=reduce_sem.at[0],
-                recv_sem=reduce_sem.at[1],
-                device_id=target,
-                device_id_type=MESH,
-            ).start()
-
-        return carry
-
-    lax.fori_loop(0, ny * 2, send_reduce, 0)
+        @pl.when(jnp.logical_not(itself))
+        def _(half=half):
+            send_reduce(y, half, device(y, half, x_hi, y))
+
     train_part(0)
     train_part(1)
     send_rows(0)
+    train_part(2)
+    train_part(3)
+    send_rows(1)
     pltpu.make_async_copy(pieces, pieces, reduce_sem.at[1]).wait()
     total = pieces[0]
     for j in range(1, nz * 2):
         total = total + pieces[j]
-    gathered[core, x_lo * groups + tile_group] = total.reshape(tile_rows, lanes).astype(BF16)
-
-    mine = gathered.at[core, x_lo * groups + tile_group]
-
-    def send_plane(j, carry):
+    gathered[core, z * 4 + x_lo * 2 + x_hi] = total.reshape(tile_rows, lanes).astype(BF16)
+
+    mine = gathered.at[core, z * 4 + x_lo * 2 + x_hi]
+    near = [k for k in range(nz) if hops(k, nz) <= 2]
+    far = [k for k in range(nz) if hops(k, nz) > 2]
+    for k, m in plane_steps:
+        sems = plane_sem.at[1 if k in near else 2]
         pltpu.make_async_remote_copy(
             src_ref=mine,
             dst_ref=mine,
             send_sem=plane_sem.at[0],
-            recv_sem=plane_sem.at[1],
-            device_id=plane_partner(j),
+            recv_sem=sems,
+            device_id=plane_partner(k, m),
             device_id_type=MESH,
         ).start()
-        return carry
-
-    lax.fori_loop(1, plane, send_plane, 0)
-    train_part(2)
-    train_part(3)
-    send_rows(1)
-    others = gathered.at[0, pl.ds(0, plane - 1)]
-    pltpu.make_async_copy(others, others, plane_sem.at[1]).wait()
-
-    sib_copy = pltpu.make_async_remote_copy(
-        src_ref=gathered.at[core],
-        dst_ref=gathered.at[core],
-        send_sem=sib_sem.at[0],
-        recv_sem=sib_sem.at[1],
-        device_id=sibling,
-        device_id_type=MESH,
-    )
-    sib_copy.start()
+
+    def forward(k):
+        window = gathered.at[core, pl.ds(z_at[k] * 4, 4)]
+        pltpu.make_async_remote_copy(
+            src_ref=window,
+            dst_ref=window,
+            send_sem=sib_sem.at[0],
+            recv_sem=sib_sem.at[1],
+            device_id=sibling,
+            device_id_type=MESH,
+        ).start()
+
+    arrived = gathered.at[0, pl.ds(0, len(near) * 4 - 1)]
+    pltpu.make_async_copy(arrived, arrived, plane_sem.at[1]).wait()
+    for k in near:
+        forward(k)
+    if far:
+        arrived = gathered.at[0, pl.ds(0, len(far) * 4)]
+        pltpu.make_async_copy(arrived, arrived, plane_sem.at[2]).wait()
+        for k in far:
+            forward(k)
     received = rows_all.at[:, pl.ds(0, ny - 1)]
     pltpu.make_async_copy(received, received, rows_sem.at[1]).wait()
 
@@ -299,7 +306,9 @@
     def product(side):
         result = None
         for xl in range(2):
-            queries = gathered[side, pl.ds(xl * groups, groups)].reshape(groups * tile_rows, lanes)
+            queries = jnp.concatenate(
+                [gathered[side, i * 4 + xl * 2 + xh] for i in range(nz) for xh in range(2)], axis=0
+            )
             documents = rows_all[pl.ds(side * (slab // 2) + xl * 2, 2)].reshape(2 * ring_docs, lanes)
             term = lax.dot_general(
                 queries, documents, (((1,), (1,)), ((), ())), preferred_element_type=F32
@@ -309,28 +318,26 @@
         return (result[:, 0, :, :ring_docs] + result[:, 1, :, ring_docs:]) * score_norm
 
     first = product(core)
-    sib_copy.wait_recv()
+    half_tiles = gathered.at[0]
+    pltpu.make_async_copy(half_tiles, half_tiles, sib_sem.at[1]).wait()
     score_send[...] = first + product(1 - core)
 
-    def send_scores(j, carry):
-        other, target = score_partner(j)
+    for k, m in score_steps:
+        dxh, dy, target = score_partner(k, m)
         pltpu.make_async_remote_copy(
-            src_ref=score_send.at[other],
+            src_ref=score_send.at[dy * 2 + dxh],
             dst_ref=score_recv.at[query],
             send_sem=score_sem.at[0],
             recv_sem=score_sem.at[1],
             device_id=target,
             device_id_type=MESH,
         ).start()
-        return carry
-
-    lax.fori_loop(1, groups, send_scores, 0)
-    score_recv[query] = score_send[query]
-
-    sib_copy.wait_send()
+    score_recv[query] = score_send[y * 2 + x_hi]
+
+    pltpu.make_async_copy(half_tiles, half_tiles, sib_sem.at[0]).wait()
+    others = gathered.at[0, pl.ds(0, len(plane_steps))]
     pltpu.make_async_copy(others, others, plane_sem.at[0]).wait()
     pltpu.make_async_copy(received, received, rows_sem.at[0]).wait()
-    own_tile = y == z
     sent = pieces.at[pl.ds(0, nz * 2 - 1)]
 
     @pl.when(own_tile)
@@ -388,7 +395,7 @@
             pltpu.VMEM((ny, 2, slab // 2, query_docs, lanes), F32),
             pltpu.VMEM((ny, slab // 2, query_docs, lanes), F32),
             pltpu.VMEM((nz * 2, 2, query_docs, lanes), F32),
-            pltpu.VMEM((2, 2 * groups, tile_rows, lanes), BF16),
+            pltpu.VMEM((2, nz * 4, tile_rows, lanes), BF16),
             pltpu.VMEM((rank, train_docs, lanes), F32),
             pltpu.VMEM((rank, batches, train_docs // batches, lanes), BF16),
             pltpu.VMEM((slab, ny, batches, train_docs // batches, lanes), BF16),
@@ -399,7 +406,7 @@
             dma((5,)),
             dma((2,)),
             dma((2,)),
-            dma((2,)),
+            dma((3,)),
             dma((2,)),
             dma((2,)),
             dma((2,)),

time: 46.6 us -> 43 us (0.923)
  the two profiles are of different devices: /device:TPU:8 before, /device:TPU:1 now
where the time goes in v3:
time: 43 us; the launch traced here: 42.7 us
  Pallas kernels  41.4 us (96%)
  local copies, waits for them, and re-layouts  1.32 us (3%)
    pallas_call x1, Pallas kernels, on_device(): pl.pallas_call(functools.partial(kernel, nz, ny, score_norm, train_norm,...  41.4 us
    unnamed x1, local copies, waits for them, and re-layouts  1.32 us

profile of v3, /device:TPU:1, one launch (start us, length us, event | category | flops | bytes accessed | tf_op | source)
XLA Modules:
  0.0 42.7 jit_solution(4960808057185626382)
XLA Ops:
  0.0 41.4 %shard_map.73 = f32[8,512]{1,0:T(8,128)} custom-call(bf16[32,2,256,128]{3,2,1,0:T(8,128)(2,1)} %train_hbm.1, s32[32]{0:T(128)} %train_len_hbm.1, bf16[8,2,256,128]{3,2,1,0:T(8,128)(2,1)} %query_hbm.1, s32[8]{0:T(128)} %query_len_hbm.1, f32[2,64,64]{2,1,0:T(8,128)} %basis_out_hbm.1, f32[2,64,64]{2,1,0:T(8,128)} %basis_in_hbm.1, f32[2,64,64]{2,1,0:T(8,128)} %eigenvalues_hbm.1), custom_call_target="tpu_custom_call" | custom-call | flops 400000000 | bytes 6000000 | tf_op jit(solution)/shard_map/pallas_call | solution.py:379
  41.4 1.3 %copy.9 = f32[512,8]{0,1:T(8,128)} copy(f32[512,8]{0,1:T(8,128)} %bitcast.1) | data formatting | bytes 32768

commit v4 on v3

--- a/solution.py
+++ b/solution.py
@@ -28,7 +28,7 @@
     out_ref,
     train_buf, train_len, query_buf, query_len, basis_out, basis_in, eigenvalues,
     right_ref, left_ref, scale_ref,
-    partial, sibling_part, pieces, gathered, rotated, rows_own, rows_all, score_send, score_recv,
+    partial, sibling_part, sums_ref, pieces, gathered, rotated, rows_own, rows_all, score_send, score_recv,
     load_sem, query_sem, small_sem, pair_sem, reduce_sem, plane_sem, sib_sem, rows_sem, score_sem,
 ):
     rank = basis_in.shape[1]
@@ -75,6 +75,25 @@
 
     load_query = pltpu.make_async_copy(query_hbm, query_buf, query_sem)
     load_query.start()
+    barrier = pltpu.get_barrier_semaphore()
+
+    def greet(target):
+        pl.semaphore_signal(barrier, inc=1, device_id=target, device_id_type=MESH)
+
+    own_tile = y == z
+    for k in sorted(range(nz), key=lambda k: -hops(k, nz)):
+        for half in range(2):
+            source, group = device(z_at[k], half, x_hi, z)
+            if k == 0:
+                source = source + jnp.where(own_tile & (x_lo == half), 1 - 2 * core, 0)
+            greet((source, group))
+    for k, m in score_steps:
+        greet(score_partner(k, m)[2])
+    for k, m in plane_steps:
+        greet(plane_partner(k, m))
+    greet(sibling)
+    greetings = 1 + nz * 2 + len(plane_steps) + len(score_steps)
+
     small = [
         pltpu.make_async_copy(src, dst, small_sem.at[i])
         for i, (src, dst) in enumerate(
@@ -97,25 +116,6 @@
         loads.append(pltpu.make_async_copy(train_hbm.at[window], train_buf.at[window], load_sem.at[i]))
         loads[-1].start()
 
-    barrier = pltpu.get_barrier_semaphore()
-
-    def greet(target):
-        pl.semaphore_signal(barrier, inc=1, device_id=target, device_id_type=MESH)
-
-    own_tile = y == z
-    for k in range(nz):
-        for half in range(2):
-            source, group = device(z_at[k], half, x_hi, z)
-            if k == 0:
-                source = source + jnp.where(own_tile & (x_lo == half), 1 - 2 * core, 0)
-            greet((source, group))
-    for k, m in plane_steps:
-        greet(plane_partner(k, m))
-    for k, m in score_steps:
-        greet(score_partner(k, m)[2])
-    greet(sibling)
-    greetings = 1 + nz * 2 + len(plane_steps) + len(score_steps)
-
     for copy in small:
         copy.wait()
     zero = jnp.zeros((rank, rank), F32)
@@ -224,12 +224,14 @@
             ).start()
         rows_all[:, y, i] = rows_own[pl.ds(y * slab, slab), i]
 
+    train_part(0)
     pair_copy.wait()
-    sibling_part[...] = sibling_part[...] + partial[:, core]
+    sums = sibling_part[...] + partial[:, core]
+    sums_ref[...] = sums.reshape(ny, 2, tile_rows, lanes).astype(BF16)
 
     def send_reduce(s, half, target):
         pltpu.make_async_remote_copy(
-            src_ref=sibling_part.at[s, pl.ds(half * 2, 2)],
+            src_ref=sums_ref.at[s, half],
             dst_ref=pieces.at[z * 2 + x_lo],
             send_sem=reduce_sem.at[0],
             recv_sem=reduce_sem.at[1],
@@ -245,35 +247,32 @@
 
         @pl.when(itself)
         def _(half=half):
-            src, dst = sibling_part.at[y, pl.ds(half * 2, 2)], pieces.at[z * 2 + x_lo]
+            src, dst = sums_ref.at[y, half], pieces.at[z * 2 + x_lo]
             pltpu.make_async_copy(src, dst, reduce_sem.at[1]).start()
 
         @pl.when(jnp.logical_not(itself))
         def _(half=half):
             send_reduce(y, half, device(y, half, x_hi, y))
 
-    train_part(0)
     train_part(1)
     send_rows(0)
     train_part(2)
     train_part(3)
     send_rows(1)
     pltpu.make_async_copy(pieces, pieces, reduce_sem.at[1]).wait()
-    total = pieces[0]
+    total = pieces[0].astype(F32)
     for j in range(1, nz * 2):
-        total = total + pieces[j]
-    gathered[core, z * 4 + x_lo * 2 + x_hi] = total.reshape(tile_rows, lanes).astype(BF16)
+        total = total + pieces[j].astype(F32)
+    gathered[core, z * 4 + x_lo * 2 + x_hi] = total.astype(BF16)
 
     mine = gathered.at[core, z * 4 + x_lo * 2 + x_hi]
-    near = [k for k in range(nz) if hops(k, nz) <= 2]
-    far = [k for k in range(nz) if hops(k, nz) > 2]
+    distances = nz // 2 + 1
     for k, m in plane_steps:
-        sems = plane_sem.at[1 if k in near else 2]
         pltpu.make_async_remote_copy(
             src_ref=mine,
             dst_ref=mine,
             send_sem=plane_sem.at[0],
-            recv_sem=sems,
+            recv_sem=plane_sem.at[1 + hops(k, nz)],
             device_id=plane_partner(k, m),
             device_id_type=MESH,
         ).start()
@@ -289,14 +288,11 @@
             device_id_type=MESH,
         ).start()
 
-    arrived = gathered.at[0, pl.ds(0, len(near) * 4 - 1)]
-    pltpu.make_async_copy(arrived, arrived, plane_sem.at[1]).wait()
-    for k in near:
-        forward(k)
-    if far:
-        arrived = gathered.at[0, pl.ds(0, len(far) * 4)]
-        pltpu.make_async_copy(arrived, arrived, plane_sem.at[2]).wait()
-        for k in far:
+    for distance in range(distances):
+        places = [k for k in range(nz) if hops(k, nz) == distance]
+        arrived = gathered.at[0, pl.ds(0, len(places) * 4 - (distance == 0))]
+        pltpu.make_async_copy(arrived, arrived, plane_sem.at[1 + distance]).wait()
+        for k in places:
             forward(k)
     received = rows_all.at[:, pl.ds(0, ny - 1)]
     pltpu.make_async_copy(received, received, rows_sem.at[1]).wait()
@@ -320,7 +316,9 @@
     first = product(core)
     half_tiles = gathered.at[0]
     pltpu.make_async_copy(half_tiles, half_tiles, sib_sem.at[1]).wait()
-    score_send[...] = first + product(1 - core)
+    scores = first + product(1 - core)
+    width = ring_docs // 2
+    score_send[...] = jnp.concatenate([scores[:, :, :width], scores[:, :, width:]], axis=1).astype(BF16)
 
     for k, m in score_steps:
         dxh, dy, target = score_partner(k, m)
@@ -351,10 +349,11 @@
     blocks = score_recv.at[pl.ds(0, groups - 1)]
     pltpu.make_async_copy(blocks, blocks, score_sem.at[1]).wait()
     for side in range(2):
-        value = score_recv[side * ny]
+        value = score_recv[side * ny].astype(F32)
         for k in range(1, ny):
-            value = value + score_recv[side * ny + k]
-        out_ref[:, side * ring_docs:(side + 1) * ring_docs] = value
+            value = value + score_recv[side * ny + k].astype(F32)
+        out_ref[:, side * ring_docs:side * ring_docs + width] = value[:query_docs]
+        out_ref[:, side * ring_docs + width:(side + 1) * ring_docs] = value[query_docs:]
     pltpu.make_async_copy(blocks, blocks, score_sem.at[0]).wait()
 
 
@@ -394,19 +393,20 @@
             pltpu.VMEM((rank, lanes), F32),
             pltpu.VMEM((ny, 2, slab // 2, query_docs, lanes), F32),
             pltpu.VMEM((ny, slab // 2, query_docs, lanes), F32),
-            pltpu.VMEM((nz * 2, 2, query_docs, lanes), F32),
+            pltpu.VMEM((ny, 2, tile_rows, lanes), BF16),
+            pltpu.VMEM((nz * 2, tile_rows, lanes), BF16),
             pltpu.VMEM((2, nz * 4, tile_rows, lanes), BF16),
             pltpu.VMEM((rank, train_docs, lanes), F32),
             pltpu.VMEM((rank, batches, train_docs // batches, lanes), BF16),
             pltpu.VMEM((slab, ny, batches, train_docs // batches, lanes), BF16),
-            pltpu.VMEM((groups, query_docs, ny * train_docs), F32),
-            pltpu.VMEM((groups, query_docs, ny * train_docs), F32),
+            pltpu.VMEM((groups, tile_rows, ny * train_docs // 2), BF16),
+            pltpu.VMEM((groups, tile_rows, ny * train_docs // 2), BF16),
             dma((4,)),
             dma,
             dma((5,)),
             dma((2,)),
             dma((2,)),
-            dma((3,)),
+            dma((nz // 2 + 2,)),
             dma((2,)),
             dma((2,)),
             dma((2,)),

time: 43 us -> 40.4 us (0.940)
  Pallas kernels: 41.4 us -> 38.9 us
    pallas_call x1, Pallas kernels: 41.4 us -> 38.9 us  [on_device(): pl.pallas_call(functools.partial(kernel, nz, ny, score_norm, train_norm,...]
where the time goes in v4:
time: 40.4 us; the launch traced here: 40.2 us
  Pallas kernels  38.9 us (96%)
  local copies, waits for them, and re-layouts  1.32 us (3%)
    pallas_call x1, Pallas kernels, on_device(): pl.pallas_call(functools.partial(kernel, nz, ny, score_norm, train_norm,...  38.9 us
    unnamed x1, local copies, waits for them, and re-layouts  1.32 us

profile of v4, /device:TPU:1, one launch (start us, length us, event | category | flops | bytes accessed | tf_op | source)
XLA Modules:
  0.0 40.2 jit_solution(13109825439115586987)
XLA Ops:
  0.0 38.9 %shard_map.73 = f32[8,512]{1,0:T(8,128)} custom-call(bf16[32,2,256,128]{3,2,1,0:T(8,128)(2,1)} %train_hbm.1, s32[32]{0:T(128)} %train_len_hbm.1, bf16[8,2,256,128]{3,2,1,0:T(8,128)(2,1)} %query_hbm.1, s32[8]{0:T(128)} %query_len_hbm.1, f32[2,64,64]{2,1,0:T(8,128)} %basis_out_hbm.1, f32[2,64,64]{2,1,0:T(8,128)} %basis_in_hbm.1, f32[2,64,64]{2,1,0:T(8,128)} %eigenvalues_hbm.1), custom_call_target="tpu_custom_call" | custom-call | flops 400000000 | bytes 6000000 | tf_op jit(solution)/shard_map/pallas_call | solution.py:378
  38.9 1.3 %copy.9 = f32[512,8]{0,1:T(8,128)} copy(f32[512,8]{0,1:T(8,128)} %bitcast.1) | data formatting | bytes 32768

commit v5 on v4

--- a/solution.py
+++ b/solution.py
@@ -75,25 +75,6 @@
 
     load_query = pltpu.make_async_copy(query_hbm, query_buf, query_sem)
     load_query.start()
-    barrier = pltpu.get_barrier_semaphore()
-
-    def greet(target):
-        pl.semaphore_signal(barrier, inc=1, device_id=target, device_id_type=MESH)
-
-    own_tile = y == z
-    for k in sorted(range(nz), key=lambda k: -hops(k, nz)):
-        for half in range(2):
-            source, group = device(z_at[k], half, x_hi, z)
-            if k == 0:
-                source = source + jnp.where(own_tile & (x_lo == half), 1 - 2 * core, 0)
-            greet((source, group))
-    for k, m in score_steps:
-        greet(score_partner(k, m)[2])
-    for k, m in plane_steps:
-        greet(plane_partner(k, m))
-    greet(sibling)
-    greetings = 1 + nz * 2 + len(plane_steps) + len(score_steps)
-
     small = [
         pltpu.make_async_copy(src, dst, small_sem.at[i])
         for i, (src, dst) in enumerate(
@@ -108,6 +89,25 @@
     ]
     for copy in small:
         copy.start()
+    barrier = pltpu.get_barrier_semaphore()
+
+    def greet(target):
+        pl.semaphore_signal(barrier, inc=1, device_id=target, device_id_type=MESH)
+
+    own_tile = y == z
+    for k in sorted(range(nz), key=lambda k: -hops(k, nz)):
+        for half in range(2):
+            source, group = device(z_at[k], half, x_hi, z)
+            if k == 0:
+                source = source + jnp.where(own_tile & (x_lo == half), 1 - 2 * core, 0)
+            greet((source, group))
+    for k, m in score_steps:
+        greet(score_partner(k, m)[2])
+    for k, m in plane_steps:
+        greet(plane_partner(k, m))
+    greet(sibling)
+    greetings = 1 + nz * 2 + len(plane_steps) + len(score_steps)
+
     parts = load_sem.shape[0]
     part_docs = train_docs // parts
     loads = []
@@ -167,7 +167,7 @@
         return results
 
     load_query.wait()
-    query_batch = 4
+    query_batch = 8
 
     def query_step(step, carry):
         summed = []
@@ -266,13 +266,15 @@
     gathered[core, z * 4 + x_lo * 2 + x_hi] = total.astype(BF16)
 
     mine = gathered.at[core, z * 4 + x_lo * 2 + x_hi]
-    distances = nz // 2 + 1
+    def ranges(k):
+        return int(hops(k, nz) > nz // 4)
+
     for k, m in plane_steps:
         pltpu.make_async_remote_copy(
             src_ref=mine,
             dst_ref=mine,
             send_sem=plane_sem.at[0],
-            recv_sem=plane_sem.at[1 + hops(k, nz)],
+            recv_sem=plane_sem.at[1 + ranges(k)],
             device_id=plane_partner(k, m),
             device_id_type=MESH,
         ).start()
@@ -288,10 +290,10 @@
             device_id_type=MESH,
         ).start()
 
-    for distance in range(distances):
-        places = [k for k in range(nz) if hops(k, nz) == distance]
-        arrived = gathered.at[0, pl.ds(0, len(places) * 4 - (distance == 0))]
-        pltpu.make_async_copy(arrived, arrived, plane_sem.at[1 + distance]).wait()
+    for group in range(2):
+        places = [k for k in range(nz) if ranges(k) == group]
+        arrived = gathered.at[0, pl.ds(0, len(places) * 4 - (group == 0))]
+        pltpu.make_async_copy(arrived, arrived, plane_sem.at[1 + group]).wait()
         for k in places:
             forward(k)
     received = rows_all.at[:, pl.ds(0, ny - 1)]
@@ -300,16 +302,16 @@
     ring_docs = ny * train_docs
 
     def product(side):
-        result = None
+        queries, documents = [], []
         for xl in range(2):
-            queries = jnp.concatenate(
-                [gathered[side, i * 4 + xl * 2 + xh] for i in range(nz) for xh in range(2)], axis=0
-            )
-            documents = rows_all[pl.ds(side * (slab // 2) + xl * 2, 2)].reshape(2 * ring_docs, lanes)
-            term = lax.dot_general(
-                queries, documents, (((1,), (1,)), ((), ())), preferred_element_type=F32
-            )
-            result = term if result is None else result + term
+            tiles = [gathered[side, i * 4 + xl * 2 + xh] for i in range(nz) for xh in range(2)]
+            queries.append(jnp.concatenate(tiles, axis=0))
+            row = side * (slab // 2) + xl * 2
+            documents.append(rows_all[pl.ds(row, 2)].reshape(2 * ring_docs, lanes))
+        result = lax.dot_general(
+            jnp.concatenate(queries, axis=1), jnp.concatenate(documents, axis=1),
+            (((1,), (1,)), ((), ())), preferred_element_type=F32,
+        )
         result = result.reshape(groups, 2, query_docs, 2 * ring_docs)
         return (result[:, 0, :, :ring_docs] + result[:, 1, :, ring_docs:]) * score_norm
 

time: 40.4 us -> 40.3 us (level)
  no operation moved by 1% of the time
where the time goes in v5:
time: 40.3 us; the launch traced here: 40.1 us
  Pallas kernels  38.7 us (96%)
  local copies, waits for them, and re-layouts  1.32 us (3%)
    pallas_call x1, Pallas kernels, on_device(): pl.pallas_call(functools.partial(kernel, nz, ny, score_norm, train_norm,...  38.7 us
    unnamed x1, local copies, waits for them, and re-layouts  1.32 us

profile of v5, /device:TPU:1, one launch (start us, length us, event | category | flops | bytes accessed | tf_op | source)
XLA Modules:
  0.0 40.1 jit_solution(8615459002574369648)
XLA Ops:
  0.0 38.7 %shard_map.73 = f32[8,512]{1,0:T(8,128)} custom-call(bf16[32,2,256,128]{3,2,1,0:T(8,128)(2,1)} %train_hbm.1, s32[32]{0:T(128)} %train_len_hbm.1, bf16[8,2,256,128]{3,2,1,0:T(8,128)(2,1)} %query_hbm.1, s32[8]{0:T(128)} %query_len_hbm.1, f32[2,64,64]{2,1,0:T(8,128)} %basis_out_hbm.1, f32[2,64,64]{2,1,0:T(8,128)} %basis_in_hbm.1, f32[2,64,64]{2,1,0:T(8,128)} %eigenvalues_hbm.1), custom_call_target="tpu_custom_call" | custom-call | flops 400000000 | bytes 6000000 | tf_op jit(solution)/shard_map/pallas_call | solution.py:380
  38.8 1.3 %copy.9 = f32[512,8]{0,1:T(8,128)} copy(f32[512,8]{0,1:T(8,128)} %bitcast.1) | data formatting | bytes 32768

commit v6 on v5

--- a/solution.py
+++ b/solution.py
@@ -301,10 +301,13 @@
 
     ring_docs = ny * train_docs
 
-    def product(side):
+    def product(side, steps):
         queries, documents = [], []
         for xl in range(2):
-            tiles = [gathered[side, i * 4 + xl * 2 + xh] for i in range(nz) for xh in range(2)]
+            tiles = []
+            for k, m in steps:
+                dxh, dy, _ = score_partner(k, m)
+                tiles.append(gathered[side, dy * 4 + xl * 2 + dxh])
             queries.append(jnp.concatenate(tiles, axis=0))
             row = side * (slab // 2) + xl * 2
             documents.append(rows_all[pl.ds(row, 2)].reshape(2 * ring_docs, lanes))
@@ -312,27 +315,33 @@
             jnp.concatenate(queries, axis=1), jnp.concatenate(documents, axis=1),
             (((1,), (1,)), ((), ())), preferred_element_type=F32,
         )
-        result = result.reshape(groups, 2, query_docs, 2 * ring_docs)
+        result = result.reshape(len(steps), 2, query_docs, 2 * ring_docs)
         return (result[:, 0, :, :ring_docs] + result[:, 1, :, ring_docs:]) * score_norm
 
-    first = product(core)
+    all_steps = score_steps + [(0, 0)]
+    step_halves = [all_steps[:groups // 2], all_steps[groups // 2:]]
+    firsts = [product(core, steps) for steps in step_halves]
     half_tiles = gathered.at[0]
     pltpu.make_async_copy(half_tiles, half_tiles, sib_sem.at[1]).wait()
-    scores = first + product(1 - core)
     width = ring_docs // 2
-    score_send[...] = jnp.concatenate([scores[:, :, :width], scores[:, :, width:]], axis=1).astype(BF16)
-
-    for k, m in score_steps:
-        dxh, dy, target = score_partner(k, m)
-        pltpu.make_async_remote_copy(
-            src_ref=score_send.at[dy * 2 + dxh],
-            dst_ref=score_recv.at[query],
-            send_sem=score_sem.at[0],
-            recv_sem=score_sem.at[1],
-            device_id=target,
-            device_id_type=MESH,
-        ).start()
-    score_recv[query] = score_send[y * 2 + x_hi]
+    for part, steps in enumerate(step_halves):
+        scores = firsts[part] + product(1 - core, steps)
+        slot = part * (groups // 2)
+        score_send[slot:slot + len(steps)] = jnp.concatenate(
+            [scores[:, :, :width], scores[:, :, width:]], axis=1
+        ).astype(BF16)
+        for i, (k, m) in enumerate(steps):
+            if k == 0 and m == 0:
+                score_recv[query] = score_send[slot + i]
+                continue
+            pltpu.make_async_remote_copy(
+                src_ref=score_send.at[slot + i],
+                dst_ref=score_recv.at[query],
+                send_sem=score_sem.at[0],
+                recv_sem=score_sem.at[1],
+                device_id=score_partner(k, m)[2],
+                device_id_type=MESH,
+            ).start()
 
     pltpu.make_async_copy(half_tiles, half_tiles, sib_sem.at[0]).wait()
     others = gathered.at[0, pl.ds(0, len(plane_steps))]

time: 40.3 us -> 40.3 us (level)
  no operation moved by 1% of the time
where the time goes in v6:
time: 40.3 us; the launch traced here: 40.1 us
  Pallas kernels  38.7 us (96%)
  local copies, waits for them, and re-layouts  1.32 us (3%)
    pallas_call x1, Pallas kernels, on_device(): pl.pallas_call(functools.partial(kernel, nz, ny, score_norm, train_norm,...  38.7 us
    unnamed x1, local copies, waits for them, and re-layouts  1.32 us

profile of v6, /device:TPU:1, one launch (start us, length us, event | category | flops | bytes accessed | tf_op | source)
XLA Modules:
  0.0 40.1 jit_solution(4478094910329616980)
XLA Ops:
  0.0 38.7 %shard_map.73 = f32[8,512]{1,0:T(8,128)} custom-call(bf16[32,2,256,128]{3,2,1,0:T(8,128)(2,1)} %train_hbm.1, s32[32]{0:T(128)} %train_len_hbm.1, bf16[8,2,256,128]{3,2,1,0:T(8,128)(2,1)} %query_hbm.1, s32[8]{0:T(128)} %query_len_hbm.1, f32[2,64,64]{2,1,0:T(8,128)} %basis_out_hbm.1, f32[2,64,64]{2,1,0:T(8,128)} %basis_in_hbm.1, f32[2,64,64]{2,1,0:T(8,128)} %eigenvalues_hbm.1), custom_call_target="tpu_custom_call" | custom-call | flops 400000000 | bytes 6000000 | tf_op jit(solution)/shard_map/pallas_call | solution.py:389
  38.7 1.3 %copy.9 = f32[512,8]{0,1:T(8,128)} copy(f32[512,8]{0,1:T(8,128)} %bitcast.1) | data formatting | bytes 32768
